TPU v7x, 32 devices: a whole 2x2x4 slice. The times are simulated.
32 devices in a mesh: trench: 8 (over y, x, core), tblock: 4 (over z).
Axes of the slice: x: 2, y: 2, z: 4, core: 2. Of those that a mesh axis runs over, the one named last changes fastest.
Arguments:
- adjoint_eta: float32 [4, 30, 128, 512], P('tblock', None, 'trench'), may hold values from -6 to 6
- adjoint_flow: float32 [4, 30, 128, 512], P('tblock', None, 'trench'), may hold values from -6 to 6
- residual: float32 [4, 8, 8, 4, 32], P('tblock', 'trench'), may hold values from -6 to 6
- sensor_cell: int32 [8, 8, 32], replicated, may hold values from 0 to 8191
- sensor_count: int32 [8, 8], replicated, may hold values from 0 to 32, as said below
- depth_class: int32 [128, 512], P('trench'), may hold values from 0 to 7
- speed_table: float32 [8], replicated, may hold values from 0.1 to 0.3
- damping: float32 [30], replicated, may hold values from 0.6 to 1
- profile: float32 [30], replicated, may hold values from 0.3 to 1
- band_weight: float32 [8], replicated, may hold values from 0.3 to 1
Outputs:
- uplift_grad: float32 [16, 128, 512], P(None, ('trench', 'tblock'))
Inputs may be any that keep to these rules, and one draw needn't show every extreme that they name: `sensor_cell`: column index inside the owning tile, row times 512 plus column. `sensor_count`: in every draw some owning tile receives 32 live slots from every source tile.
All inputs are finite; a program needn't handle non-finite values.
Results may differ from a plain program's by a relative error of at most 0.0001.
Values sent between devices are 32-bit elements; how exact they have to be, the bound alone decides.
No kernel may reach another device: no remote copies, remote signals or barrier semaphores. Data moves between devices by JAX's collectives and lax.ppermute only.
A program may use at most 64 MiB of HBM per device.

v0:
```python
import functools
import math

import jax
import jax.numpy as jnp
from jax import lax
from jax.experimental import pallas as pl
from jax.experimental.pallas import tpu as pltpu
from jax.sharding import PartitionSpec as P

VERT = 0.2
STEPS = 4
PAD = 8
VMEM = pltpu.VMEM
SMEM = pltpu.SMEM
LIMIT = 32 * 1024 * 1024

SHIFT = 1.2

FIELDS = [(4, 4), (4, 3), (4, 2), (3, 2), (4, 1), (3, 1), (2, 1), (4, 0), (3, 0), (2, 0), (1, 0)]
HALO = [4, 3, 2, 2, 1, 1, 1]
HALO_AT = [0, 4, 7, 9, 11, 12, 13]
CEL_AT = 14
CEL_HALO = 3
ROWS = 17


def split(x):
    hi = x.astype(jnp.bfloat16)
    return hi, (x - hi.astype(jnp.float32)).astype(jnp.bfloat16)


def dot(a, b, dims=((1,), (0,))):
    return lax.dot_general(a, b, (dims, ((), ())), preferred_element_type=jnp.float32)


def contract_kernel(
    eta, flow, depth, table, damping, profile, cells, count, residual,
    fields, edges, outer, cel, coef, hot, places,
    eta_v, flow_v, depth_v, table_s, damping_v, profile_v, cells_v, count_s, own, sems,
):
    levels, rows, across = eta.shape[1:]
    halves = rows // 8
    copies = []

    def fetch(src, dst):
        copy = pltpu.make_async_copy(src, dst, sems.at[len(copies)])
        copy.start()
        copies.append(copy)
        return copy

    small = [fetch(damping, damping_v), fetch(profile, profile_v), fetch(table, table_s), fetch(depth, depth_v)]
    small += [fetch(cells, cells_v), fetch(count, count_s), fetch(residual, own)]
    large = []
    for h in range(halves):
        cut = pl.ds(8 * h, 8)
        large.append(fetch(eta.at[0, :, cut, :], eta_v.at[h]))
        large.append(fetch(flow.at[0, :, cut, :], flow_v.at[h]))
    for copy in small:
        copy.wait()

    classes = depth_v[...]
    speed = jnp.zeros(classes.shape, jnp.float32)
    for c in range(table_s.shape[0]):
        speed = jnp.where(classes == c, table_s[c], speed)
    cel[...] = speed

    lane = lax.broadcasted_iota(jnp.int32, (8, 128), 1)
    sub = lax.broadcasted_iota(jnp.int32, (8, 128), 0)
    inside = lane < levels
    fill = jnp.zeros((1, 128 - levels), jnp.float32)
    keep = jnp.broadcast_to(jnp.concatenate([damping_v[...], fill], axis=1), (8, 128))
    weight = jnp.broadcast_to(jnp.concatenate([profile_v[...], fill], axis=1), (8, 128))
    u = jnp.zeros((8, 128), jnp.float32)
    v = jnp.where(sub == 0, weight * (1.0 / math.sqrt(levels)), 0.0)
    us, vs = [u], [v]
    for r in range(STEPS):
        s = u + v
        bottom = jnp.sum(jnp.where(lane == levels - 1, s, 0.0), axis=1, keepdims=True)
        coef[8 * r : 8 * r + 8, :] = jnp.broadcast_to(bottom, (8, coef.shape[1]))
        vertical = pltpu.roll(s, 1, 1) + pltpu.roll(s, 127, 1) - 2.0 * s
        u = jnp.where(inside, u + VERT * vertical - SHIFT * s + pltpu.roll(s, 1, 0), 0.0)
        v = s * keep
        us.append(u)
        vs.append(v)

    wide = levels * 8
    spread = (
        lax.broadcasted_iota(jnp.int32, (128, wide), 1) // 8
        == lax.broadcasted_iota(jnp.int32, (128, wide), 0)
    ).astype(jnp.bfloat16)
    count_f = len(FIELDS) + 1
    diagonal = (
        lax.broadcasted_iota(jnp.int32, (8 * count_f, wide), 1) % 8
        == lax.broadcasted_iota(jnp.int32, (8 * count_f, wide), 0) % 8
    )

    def matrix(vectors):
        blocks = [jnp.broadcast_to(vectors[n][k : k + 1, :], (8, 128)) for n, k in FIELDS]
        blocks.append(jnp.zeros((8, 128), jnp.float32))
        hi, lo = split(jnp.concatenate(blocks, axis=0))
        zero = jnp.zeros((8 * count_f, wide), jnp.float32)
        hi = jnp.where(diagonal, dot(hi, spread), zero).astype(jnp.bfloat16)
        lo = jnp.where(diagonal, dot(lo, spread), zero).astype(jnp.bfloat16)
        return hi, jnp.concatenate([hi, lo], axis=0)

    w_eta, both_eta = matrix(us)
    w_flow, both_flow = matrix(vs)

    me = lax.axis_index("trench")
    tiles, _, slots = cells_v.shape
    slot = lax.broadcasted_iota(jnp.int32, (1, slots), 1)
    listed = []
    for source in sources(me, tiles):
        for d in range(3):
            owner = me + d - 1
            inside = (owner >= 0) & (owner < tiles)
            owner = jnp.clip(owner, 0, tiles - 1)
            live = jnp.where(inside, count_s[source, owner], 0)
            listed.append(jnp.where(slot < live, cells_v[source, pl.ds(owner, 1), :], -1))
    listed = jnp.concatenate(listed, axis=1)
    tile = (lax.broadcasted_iota(jnp.int32, listed.shape, 1) // slots) % 3
    bits = across.bit_length() - 1
    at = jnp.where(listed < 0, -1, (listed >> bits) + (rows * (tile - 1) + PAD))
    places[...] = jnp.broadcast_to(at, places.shape)
    columns = listed & (across - 1)
    hot[...] = jnp.where(lax.broadcasted_iota(jnp.int32, hot.shape, 0) == columns, 1.0, 0.0).astype(jnp.bfloat16)

    for q in range(tiles // 2):
        row, lane_at = packed(q, across)
        values = residual_rows(met(me ^ 1, q, tiles), own)
        edges[row : row + STEPS, lane_at : lane_at + 128] = jnp.concatenate(
            [values, jnp.zeros((STEPS, 128 - values.shape[1]), jnp.float32)], axis=1
        )

    for h in range(halves):
        large[2 * h].wait()
        hi, lo = split(eta_v[h].reshape(wide, across))
        total = dot(both_eta, hi)
        part = dot(w_eta, lo)
        large[2 * h + 1].wait()
        hi, lo = split(flow_v[h].reshape(wide, across))
        total += dot(both_flow, hi)
        part += dot(w_flow, lo)
        part = part + total[: 8 * count_f] + total[8 * count_f :]
        for f in range(len(FIELDS)):
            fields[f, 8 * h : 8 * h + 8, :] = part[8 * f : 8 * f + 8]

    def edge(out, last):
        for f, width in enumerate(HALO):
            start = rows - width if last else 0
            out[HALO_AT[f] : HALO_AT[f] + width, :] = fields[f, start : start + width, :]
        start = rows - CEL_HALO if last else 0
        out[CEL_AT : CEL_AT + CEL_HALO, :] = cel[start : start + CEL_HALO, :]

    @pl.when(me % 2 == 0)
    def _():
        edge(edges, True)
        edge(outer, False)

    @pl.when(me % 2 == 1)
    def _():
        edge(edges, False)
        edge(outer, True)


def met(me, d, tiles):
    odd = me % 2
    chip = (me // 2 + jnp.where(odd == 1, d, tiles // 2 - d)) % (tiles // 2)
    return jnp.where(d == 0, me, 2 * chip + 1 - odd)


def sources(me, tiles):
    return [met(me, d, tiles) ^ core for d in range(tiles // 2) for core in range(2)]


def residual_rows(owner, own):
    tiles = own.shape[0]
    return jnp.concatenate([own[jnp.clip(owner + d - 1, 0, tiles - 1)] for d in range(3)], axis=1)


def packed(q, across):
    per = across // 128
    return ROWS + STEPS * (q // per), 128 * (q % per)


def both_rows(owner, q, own, edges):
    row, lane_at = packed(q, edges.shape[1])
    slots = own.shape[2]
    return jnp.concatenate(
        [residual_rows(owner, own), edges[row : row + STEPS, lane_at : lane_at + 3 * slots]], axis=1
    )


def relay_kernel(own, edges, outer, *outs):
    me = lax.axis_index("trench")
    tiles = own.shape[0]
    for d, out in enumerate(outs, 1):
        values = both_rows(met(me, d, tiles), d, own, edges)
        fill = jnp.zeros((STEPS, out.shape[1] - values.shape[1]), jnp.float32)
        out[0:STEPS, :] = jnp.concatenate([values, fill], axis=1)
        if d == 1:
            out[STEPS : STEPS + ROWS, :] = outer[...]


def advance_kernel(blocks, fields, cel, coef, hot, places, own, edges, *refs):
    cross, outs, (stage, ext, cel_ext) = refs[: -3 - blocks], refs[-3 - blocks : -3], refs[-3:]
    me = lax.axis_index("trench")
    tiles = own.shape[0]
    rows, across = cel.shape
    tall = rows + 2 * PAD
    part = rows // blocks
    odd = me % 2 == 1
    facing = me // 2 + jnp.where(odd, 1, -1)
    inner = edges[0:ROWS, :]
    outer = jnp.zeros(inner.shape, jnp.float32)
    if cross:
        outer = jnp.where((facing >= 0) & (facing < tiles // 2), cross[0][STEPS : STEPS + ROWS, :], outer)
    before = jnp.where(odd, inner, outer)
    after = jnp.where(odd, outer, inner)

    per = 6 * own.shape[2]
    values = [both_rows(me, 0, own, edges)] + [got[0:STEPS, 0:per] for got in cross]
    values = jnp.concatenate(values, axis=1)
    here = lax.broadcasted_iota(jnp.int32, (tall, values.shape[1]), 0) == places[0:1, :]
    left = jnp.concatenate([jnp.where(here, values[t : t + 1, :], 0.0) for t in range(STEPS)], axis=0)
    hi, lo = split(left)
    planes = dot(hi, hot[...], ((1,), (1,))) + dot(lo, hot[...], ((1,), (1,)))
    inject = [planes[tall * t : tall * t + tall] for t in range(STEPS)]

    def extend(store, own, at, width):
        store(0, PAD, jnp.zeros((PAD, across), jnp.float32))
        store(PAD + rows, tall, jnp.zeros((PAD, across), jnp.float32))
        store(PAD, PAD + rows, own)
        store(PAD - width, PAD, before[at : at + width])
        store(PAD + rows, PAD + rows + width, after[at : at + width])

    for f, width in enumerate(HALO):
        def store(a, b, value, f=f):
            ext[f, a:b, :] = value
        extend(store, fields[f], HALO_AT[f], width)

    def store_cel(a, b, value):
        cel_ext[a:b, :] = value
    extend(store_cel, cel[...], CEL_AT, CEL_HALO)

    lane = lax.broadcasted_iota(jnp.int32, (tall, across), 1)
    first = lane == 0
    last = lane == across - 1
    speed = cel_ext[...]

    def horizontal(z):
        around = pltpu.roll(z, 1, 0) + pltpu.roll(z, tall - 1, 0)
        around += jnp.where(first, 0.0, pltpu.roll(z, 1, 1))
        around += jnp.where(last, 0.0, pltpu.roll(z, across - 1, 1))
        return speed * (around - 4.0 * z) + SHIFT * z

    def injected(n, k, a, b):
        total = None
        for tau in range(1, n - k + 1):
            r = n - tau
            term = coef[8 * r + k : 8 * r + k + 1, :] * inject[STEPS - tau][a:b]
            total = term if total is None else total + term
        return total

    base = horizontal(ext[0])
    for n in range(1, STEPS + 1):
        z = base
        for k in range(n - 1, 0, -1):
            z = horizontal(z + ext[FIELDS.index((n, k))] + injected(n, k, 0, tall))
        own = z[PAD : PAD + rows] + fields[FIELDS.index((n, 0))] + injected(n, 0, PAD, PAD + rows)
        t = STEPS - n
        for b in range(blocks):
            stage[b, part * t : part * t + part, :] = own[part * b : part * b + part]
    block = lax.axis_index("tblock")
    for r, out in enumerate(outs):
        out[...] = stage[block ^ r]


def prior_kernel(*refs):
    gots, weight, out, whole = refs[:-3], refs[-3], refs[-2], refs[-1]
    block = lax.axis_index("tblock")
    for r, got in enumerate(reversed(gots)):
        whole[block ^ r] = got[...]
    part = out.shape[1]
    length = out.shape[0]
    width = weight.shape[0]
    if 2 * part != 8:
        series = [whole[i // STEPS, part * (i % STEPS) : part * (i % STEPS) + part, :] for i in range(length)]
        for k in range(length):
            out[k] = sum(weight[j] * series[k + j] for j in range(min(width, length - k)))
        return
    pairs = length // 2
    even = [whole[p // 2, 8 * (p % 2) : 8 * (p % 2) + 8, :] for p in range(pairs)]
    half = lax.broadcasted_iota(jnp.int32, even[0].shape, 0) < part
    turned = [pltpu.roll(x, part, 0) for x in even] + [jnp.zeros(even[0].shape, jnp.float32)]
    odd = [jnp.where(half, turned[p], turned[p + 1]) for p in range(pairs)]
    for p in range(pairs):
        total = None
        for j in range(width):
            if p + j // 2 < pairs:
                term = weight[j] * (odd if j % 2 else even)[p + j // 2]
                total = term if total is None else total + term
        out[2 * p] = total[:part]
        out[2 * p + 1] = total[part:]


def shape(*dims, dtype=jnp.float32):
    return jax.ShapeDtypeStruct(dims, dtype)


def spec(space):
    return pl.BlockSpec(memory_space=space)


def body(
    adjoint_eta,
    adjoint_flow,
    residual,
    sensor_cell,
    sensor_count,
    depth_class,
    speed_table,
    damping,
    profile,
    band_weight,
):
    tiles = lax.axis_size("trench")
    blocks = lax.axis_size("tblock")
    levels, rows, across = adjoint_eta.shape[1:]
    tall = rows + 2 * PAD
    params = pltpu.CompilerParams(vmem_limit_bytes=LIMIT)

    def swaps(parts, axis):
        devices = lax.axis_size(axis)
        moved = {r: lax.ppermute(parts[r], axis, [(i, i ^ r) for i in range(devices)]) for r in range(devices - 1, 0, -1)}
        return [parts[0]] + [moved[r] for r in range(1, devices)]

    own = residual[0, 0]
    slots = own.shape[2]
    lanes = 3 * tiles * slots

    chips = tiles // 2

    def meet(x, d):
        pairs = [(2 * c + 1, 2 * ((c + d) % chips)) for c in range(chips)]
        return lax.ppermute(x, "trench", pairs + [(j, i) for i, j in pairs])

    fields, edges, outer, cel, coef, hot, places = pl.pallas_call(
        contract_kernel,
        out_shape=(
            shape(len(FIELDS), rows, across),
            shape(ROWS + STEPS * -(-64 * tiles // across), across),
            shape(ROWS, across),
            shape(rows, across),
            shape(8 * STEPS, across),
            shape(across, lanes, dtype=jnp.bfloat16),
            shape(8, lanes, dtype=jnp.int32),
        ),
        in_specs=[spec(pltpu.HBM)] * 9,
        out_specs=(spec(VMEM),) * 7,
        scratch_shapes=[
            VMEM((rows // 8, levels, 8, across), jnp.float32),
            VMEM((rows // 8, levels, 8, across), jnp.float32),
            VMEM((rows, across), jnp.int32),
            SMEM(speed_table.shape, jnp.float32),
            VMEM((1, levels), jnp.float32),
            VMEM((1, levels), jnp.float32),
            VMEM(sensor_cell.shape, jnp.int32),
            SMEM(sensor_count.shape, jnp.int32),
            VMEM(own.shape, jnp.float32),
            pltpu.SemaphoreType.DMA((7 + 2 * (rows // 8),)),
        ],
        compiler_params=params,
        cost_estimate=pl.CostEstimate(flops=10**9, bytes_accessed=10**7, transcendentals=0),
        name="contract",
    )(
        *[
            pltpu.with_memory_space_constraint(x, pltpu.HBM)
            for x in (
                adjoint_eta, adjoint_flow, depth_class, speed_table, damping[None], profile[None],
                sensor_cell, sensor_count, own,
            )
        ]
    )

    edges = meet(edges, 0)
    relays = pl.pallas_call(
        relay_kernel,
        out_shape=[
            shape(STEPS + ROWS, across) if d == 1 else shape(STEPS, -(-6 * slots // 128) * 128)
            for d in range(1, chips)
        ],
        in_specs=[spec(VMEM)] * 3,
        out_specs=[spec(VMEM)] * (chips - 1),
        compiler_params=params,
        name="relay",
    )(own, edges, outer)
    cross = [meet(relay, d) for d, relay in enumerate(relays, 1)]
    series = pl.pallas_call(
        functools.partial(advance_kernel, blocks),
        out_shape=(shape(STEPS * rows // blocks, across),) * blocks,
        in_specs=[spec(VMEM)] * (7 + len(cross)),
        out_specs=(spec(VMEM),) * blocks,
        scratch_shapes=[
            VMEM((blocks, STEPS * rows // blocks, across), jnp.float32),
            VMEM((len(HALO), tall, across), jnp.float32),
            VMEM((tall, across), jnp.float32),
        ],
        compiler_params=params,
        name="advance",
    )(fields, cel, coef, hot, places, own, edges, *cross)
    gots = swaps(series, "tblock")
    return pl.pallas_call(
        prior_kernel,
        out_shape=shape(STEPS * blocks, rows // blocks, across),
        in_specs=[spec(VMEM)] * blocks + [spec(SMEM)],
        out_specs=spec(VMEM),
        scratch_shapes=[VMEM((blocks, STEPS * rows // blocks, across), jnp.float32)],
        compiler_params=params,
        name="prior",
    )(*reversed(gots), band_weight)


def solution(mesh):
    in_specs = (
        P("tblock", None, "trench", None),
        P("tblock", None, "trench", None),
        P("tblock", "trench", None, None, None),
        P(),
        P(),
        P("trench", None),
        P(),
        P(),
        P(),
        P(),
    )
    out_specs = P(None, ("trench", "tblock"), None)
    return jax.shard_map(body, mesh=mesh, in_specs=in_specs, out_specs=out_specs, check_vma=False)
```

profile of v0, /device:TPU:0, one launch (start us, length us, event | category | flops | bytes accessed | tf_op | source)
XLA Modules:
  0.0 22.1 jit_solution(14254865198513686785)
XLA Ops:
  0.0 0.0 copy-start
  0.0 2.5 %contract.1 = (f32[11,16,512]{2,1,0:T(8,128)S(1)}, f32[21,512]{1,0:T(8,128)S(1)}, f32[17,512]{1,0:T(8,128)S(1)}, f32[16,512]{1,0:T(8,128)S(1)}, f32[32,512]{1,0:...) custom-call(f32[1,30,16,512]{3,2,1,0:T(8,128)} %eta.1, f32[1,30,16,512]{3,2,1,0:T(8,128)} %flow.1, ...), custom_call_target="tpu_custom_call" | custom-call | flops 1000000000 | bytes 10000000 | tf_op jit(solution)/shard_map/contract/pallas_call | solution.py:349
  2.5 0.5 %collective-permute-start = (f32[21,512]{1,0:T(8,128)S(1)}, f32[21,512]{1,0:T(8,128)S(1)}, u32[]{:S(2)}, u32[]{:S(2)}) collective-permute-start(f32[21,512]{1,0:T(8,128)S(1)} %get-tuple-element.24), channel_id=1, source_target_pairs={{4,0},{12,8},{20,16},{28,24},{0,4},{8,12},{16,20},{24,28},{5,1},{1... | collective-permute-start | bytes 129032 | tf_op jit(solution)/shard_map/ppermute | solution.py:347
  3.0 0.9 %collective-permute-done.edges = f32[21,512]{1,0:T(8,128)S(1)} collective-permute-done((f32[21,512]{1,0:T(8,128)S(1)}, f32[21,512]{1,0:T(8,128)S(1)}, u32[]{:S(2)}, u32[]{:S(2)}) %collective-permute-start) | collective-permute-done | bytes 43040 | tf_op jit(solution)/shard_map/ppermute | solution.py:347
  3.9 0.0 copy-done
  3.9 0.1 relay.1
  4.0 3.6 %collective-permute-start.1 = (f32[21,512]{1,0:T(8,128)S(1)}, f32[21,512]{1,0:T(8,128)S(1)}, u32[]{:S(2)}, u32[]{:S(2)}) collective-permute-start(f32[21,512]{1,0:T(8,128)S(1)} %get-tuple-element.26), channel_id=1, source_target_pairs={{4,8},{12,16},{20,24},{28,0},{8,4},{16,12},{24,20},{0,28},{5,9},{1... | collective-permute-start | bytes 129032 | tf_op jit(solution)/shard_map/ppermute | solution.py:347
  7.7 0.5 %collective-permute-start.2 = (f32[4,256]{1,0:T(4,128)S(1)}, f32[4,256]{1,0:T(4,128)S(1)}, u32[]{:S(2)}, u32[]{:S(2)}) collective-permute-start(f32[4,256]{1,0:T(4,128)S(1)} %get-tuple-element.27), channel_id=1, source_target_pairs={{4,16},{12,24},{20,0},{28,8},{16,4},{24,12},{0,20},{8,28},{5,17},{... | collective-permute-start | bytes 12296 | tf_op jit(solution)/shard_map/ppermute | solution.py:347
  8.2 0.3 %collective-permute-start.3 = (f32[4,256]{1,0:T(4,128)S(1)}, f32[4,256]{1,0:T(4,128)S(1)}, u32[]{:S(2)}, u32[]{:S(2)}) collective-permute-start(f32[4,256]{1,0:T(4,128)S(1)} %get-tuple-element.28), channel_id=1, source_target_pairs={{4,24},{12,0},{20,8},{28,16},{24,4},{0,12},{8,20},{16,28},{5,25},{... | collective-permute-start | bytes 12296 | tf_op jit(solution)/shard_map/ppermute | solution.py:347
  8.5 2.2 %collective-permute-done.2.refs_1_ = f32[4,256]{1,0:T(4,128)S(1)} collective-permute-done((f32[4,256]{1,0:T(4,128)S(1)}, f32[4,256]{1,0:T(4,128)S(1)}, u32[]{:S(2)}, u32[]{:S(2)}) %collective-permute-start.2) | collective-permute-done | bytes 4128 | tf_op jit(solution)/shard_map/ppermute | solution.py:347
  10.7 0.5 %collective-permute-done.3.refs_2_ = f32[4,256]{1,0:T(4,128)S(1)} collective-permute-done((f32[4,256]{1,0:T(4,128)S(1)}, f32[4,256]{1,0:T(4,128)S(1)}, u32[]{:S(2)}, u32[]{:S(2)}) %collective-permute-start.3) | collective-permute-done | bytes 4128 | tf_op jit(solution)/shard_map/ppermute | solution.py:347
  11.2 0.0 collective-permute-done.1.refs_0_
  11.2 1.0 %advance.1 = (f32[16,512]{1,0:T(8,128)S(1)}, f32[16,512]{1,0:T(8,128)S(1)}, f32[16,512]{1,0:T(8,128)S(1)}, f32[16,512]{1,0:T(8,128)S(1)}) custom-call(f32[11,16,512]{2,1,0:T(8,128)S(1)} %get-tuple-element.19.fields, f32[16,512]{1,0:T(8,128)S(1)} %get-tuple-element.20.cel, f32[32,512]{1,0:T(8,128)S(1)} %get-tuple-element.21.coef, ...), custom_call_target="tpu_custom_call" | custom-call | tf_op jit(solution)/shard_map/advance/pallas_call | solution.py:400
  12.3 3.7 %collective-permute-start.4 = (f32[16,512]{1,0:T(8,128)S(1)}, f32[16,512]{1,0:T(8,128)S(1)}, u32[]{:S(2)}, u32[]{:S(2)}) collective-permute-start(f32[16,512]{1,0:T(8,128)S(1)} %get-tuple-element.29), channel_id=1, source_target_pairs={{0,3},{1,2},{2,1},{3,0},{4,7},{5,6},{6,5},{7,4},{8,11},{9,10},{10,... | collective-permute-start | bytes 98312 | tf_op jit(solution)/shard_map/ppermute | solution.py:336
  15.9 0.0 collective-permute-start.5
  15.9 0.0 copy-start.1
  15.9 0.8 %collective-permute-start.6 = (f32[16,512]{1,0:T(8,128)S(1)}, f32[16,512]{1,0:T(8,128)S(1)}, u32[]{:S(2)}, u32[]{:S(2)}) collective-permute-start(f32[16,512]{1,0:T(8,128)S(1)} %get-tuple-element.31), channel_id=1, source_target_pairs={{0,1},{1,0},{2,3},{3,2},{4,5},{5,4},{6,7},{7,6},{8,9},{9,8},{10,11... | collective-permute-start | bytes 98312 | tf_op jit(solution)/shard_map/ppermute | solution.py:336
  16.7 1.6 %collective-permute-done.4.refs_0_ = f32[16,512]{1,0:T(8,128)S(1)} collective-permute-done((f32[16,512]{1,0:T(8,128)S(1)}, f32[16,512]{1,0:T(8,128)S(1)}, u32[]{:S(2)}, u32[]{:S(2)}) %collective-permute-start.4) | collective-permute-done | bytes 32800 | tf_op jit(solution)/shard_map/ppermute | solution.py:336
  18.3 2.5 %collective-permute-done.5.refs_1_ = f32[16,512]{1,0:T(8,128)S(1)} collective-permute-done((f32[16,512]{1,0:T(8,128)S(1)}, f32[16,512]{1,0:T(8,128)S(1)}, u32[]{:S(2)}, u32[]{:S(2)}) %collective-permute-start.5) | collective-permute-done | bytes 32800 | tf_op jit(solution)/shard_map/ppermute | solution.py:336
  20.8 0.0 collective-permute-done.6.refs_2_
  20.8 0.0 copy-done.1
  20.8 1.3 %prior.1 = f32[16,4,512]{2,1,0:T(4,128)} custom-call(f32[16,512]{1,0:T(8,128)S(1)} %collective-permute-done.4.refs_0_, f32[16,512]{1,0:T(8,128)S(1)} %collective-permute-done.5.refs_1_, f32[16,512]{1,0:T(8,128)S(1)} %collective-permute-done.6.refs_2_, f32[16,512]{1,0:T(8,128)S(1)} %get-tuple-element.32.refs_3_, f32[8]{0:T(128)S(1)} %copy-done.1), custom_call_target="tpu_custom_call" | custom-call | tf_op jit(solution)/shard_map/prior/pallas_call | solution.py:414
Async XLA Ops:
  0.0 3.9 %copy-start = (f32[1,1,8,4,32]{4,3,2,1,0:T(4,128)S(1)}, f32[1,1,8,4,32]{4,3,2,1,0:T(4,128)}, u32[]{:S(2)}) copy-start(f32[1,1,8,4,32]{4,3,2,1,0:T(4,128)} %param.12) | copy-start | bytes 12292
  2.5 1.4 %collective-permute-start = (f32[21,512]{1,0:T(8,128)S(1)}, f32[21,512]{1,0:T(8,128)S(1)}, u32[]{:S(2)}, u32[]{:S(2)}) collective-permute-start(f32[21,512]{1,0:T(8,128)S(1)} %get-tuple-element.24), channel_id=1, source_target_pairs={{4,0},{12,8},{20,16},{28,24},{0,4},{8,12},{16,20},{24,28},{5,1},{1... | collective-permute-start | bytes 129032 | tf_op jit(solution)/shard_map/ppermute | solution.py:347
  4.0 7.2 %collective-permute-start.1 = (f32[21,512]{1,0:T(8,128)S(1)}, f32[21,512]{1,0:T(8,128)S(1)}, u32[]{:S(2)}, u32[]{:S(2)}) collective-permute-start(f32[21,512]{1,0:T(8,128)S(1)} %get-tuple-element.26), channel_id=1, source_target_pairs={{4,8},{12,16},{20,24},{28,0},{8,4},{16,12},{24,20},{0,28},{5,9},{1... | collective-permute-start | bytes 129032 | tf_op jit(solution)/shard_map/ppermute | solution.py:347
  7.7 3.0 %collective-permute-start.2 = (f32[4,256]{1,0:T(4,128)S(1)}, f32[4,256]{1,0:T(4,128)S(1)}, u32[]{:S(2)}, u32[]{:S(2)}) collective-permute-start(f32[4,256]{1,0:T(4,128)S(1)} %get-tuple-element.27), channel_id=1, source_target_pairs={{4,16},{12,24},{20,0},{28,8},{16,4},{24,12},{0,20},{8,28},{5,17},{... | collective-permute-start | bytes 12296 | tf_op jit(solution)/shard_map/ppermute | solution.py:347
  8.2 3.0 %collective-permute-start.3 = (f32[4,256]{1,0:T(4,128)S(1)}, f32[4,256]{1,0:T(4,128)S(1)}, u32[]{:S(2)}, u32[]{:S(2)}) collective-permute-start(f32[4,256]{1,0:T(4,128)S(1)} %get-tuple-element.28), channel_id=1, source_target_pairs={{4,24},{12,0},{20,8},{28,16},{24,4},{0,12},{8,20},{16,28},{5,25},{... | collective-permute-start | bytes 12296 | tf_op jit(solution)/shard_map/ppermute | solution.py:347
  12.3 6.0 %collective-permute-start.4 = (f32[16,512]{1,0:T(8,128)S(1)}, f32[16,512]{1,0:T(8,128)S(1)}, u32[]{:S(2)}, u32[]{:S(2)}) collective-permute-start(f32[16,512]{1,0:T(8,128)S(1)} %get-tuple-element.29), channel_id=1, source_target_pairs={{0,3},{1,2},{2,1},{3,0},{4,7},{5,6},{6,5},{7,4},{8,11},{9,10},{10,... | collective-permute-start | bytes 98312 | tf_op jit(solution)/shard_map/ppermute | solution.py:336
  15.9 4.9 %collective-permute-start.5 = (f32[16,512]{1,0:T(8,128)S(1)}, f32[16,512]{1,0:T(8,128)S(1)}, u32[]{:S(2)}, u32[]{:S(2)}) collective-permute-start(f32[16,512]{1,0:T(8,128)S(1)} %get-tuple-element.30), channel_id=1, source_target_pairs={{0,2},{1,3},{2,0},{3,1},{4,6},{5,7},{6,4},{7,5},{8,10},{9,11},{10,... | collective-permute-start | bytes 98312 | tf_op jit(solution)/shard_map/ppermute | solution.py:336
  15.9 4.9 %copy-start.1 = (f32[8]{0:T(128)S(1)}, f32[8]{0:T(128)}, u32[]{:S(2)}) copy-start(f32[8]{0:T(128)} %refs_4_.1) | copy-start | bytes 100
  15.9 4.9 %collective-permute-start.6 = (f32[16,512]{1,0:T(8,128)S(1)}, f32[16,512]{1,0:T(8,128)S(1)}, u32[]{:S(2)}, u32[]{:S(2)}) collective-permute-start(f32[16,512]{1,0:T(8,128)S(1)} %get-tuple-element.31), channel_id=1, source_target_pairs={{0,1},{1,0},{2,3},{3,2},{4,5},{5,4},{6,7},{7,6},{8,9},{9,8},{10,11... | collective-permute-start | bytes 98312 | tf_op jit(solution)/shard_map/ppermute | solution.py:336
where the time goes:
time: 22.3 us; the launch traced here: 22.1 us
  starting transfers between devices  9.41 us (42%)
  waiting for transfers between devices  7.75 us (35%)
  Pallas kernels  4.93 us (22%)
    ppermute x4, starting transfers between devices, meet(): return lax.ppermute(x, 'trench', pairs + [(j, i) for i, j in pairs])  4.95 us
    ppermute x3, starting transfers between devices, swaps(): lax.ppermute(parts[r], axis, [(i, i ^ r) for i in range(devices)])  4.45 us
    ppermute x3, waiting for transfers between devices, swaps(): lax.ppermute(parts[r], axis, [(i, i ^ r) for i in range(devices)])  4.11 us
    ppermute x4, waiting for transfers between devices, meet(): return lax.ppermute(x, 'trench', pairs + [(j, i) for i, j in pairs])  3.64 us
    pallas_call x1, Pallas kernels, body(): pl.pallas_call(contract_kernel, out_shape=(shape(len(FIELDS), rows, acros...  2.52 us
    pallas_call x1, Pallas kernels, body(): pl.pallas_call(prior_kernel, out_shape=shape(STEPS * blocks, rows // bloc...  1.28 us
    pallas_call x1, Pallas kernels, body(): pl.pallas_call(functools.partial(advance_kernel, blocks), out_shape=(shap...  1.02 us
  transfers between devices with their start and end apart: 7, of which 5 were waited for; matrix products, arithmetic and copies ran while one was open for 0% of the time, Pallas kernels for 0%

commit v1 on v0

--- a/solution.py
+++ b/solution.py
@@ -35,9 +35,9 @@
 
 
 def contract_kernel(
-    eta, flow, depth, table, damping, profile, cells, count, residual,
-    fields, edges, outer, cel, coef, hot, places,
-    eta_v, flow_v, depth_v, table_s, damping_v, profile_v, cells_v, count_s, own, sems,
+    eta, flow, depth, table, damping, profile, band, residual,
+    fields, inner, outer, cel, coef, factor, own,
+    eta_v, flow_v, depth_v, table_s, damping_v, profile_v, band_v, sems,
 ):
     levels, rows, across = eta.shape[1:]
     halves = rows // 8
@@ -50,7 +50,7 @@
         return copy
 
     small = [fetch(damping, damping_v), fetch(profile, profile_v), fetch(table, table_s), fetch(depth, depth_v)]
-    small += [fetch(cells, cells_v), fetch(count, count_s), fetch(residual, own)]
+    small += [fetch(band, band_v), fetch(residual, own)]
     large = []
     for h in range(halves):
         cut = pl.ds(8 * h, 8)
@@ -64,6 +64,8 @@
     for c in range(table_s.shape[0]):
         speed = jnp.where(classes == c, table_s[c], speed)
     cel[...] = speed
+    for j in range(factor.shape[0]):
+        factor[j : j + 1, :] = jnp.broadcast_to(band_v[:, j : j + 1], (1, across))
 
     lane = lax.broadcasted_iota(jnp.int32, (8, 128), 1)
     sub = lax.broadcasted_iota(jnp.int32, (8, 128), 0)
@@ -107,32 +109,6 @@
     w_eta, both_eta = matrix(us)
     w_flow, both_flow = matrix(vs)
 
-    me = lax.axis_index("trench")
-    tiles, _, slots = cells_v.shape
-    slot = lax.broadcasted_iota(jnp.int32, (1, slots), 1)
-    listed = []
-    for source in sources(me, tiles):
-        for d in range(3):
-            owner = me + d - 1
-            inside = (owner >= 0) & (owner < tiles)
-            owner = jnp.clip(owner, 0, tiles - 1)
-            live = jnp.where(inside, count_s[source, owner], 0)
-            listed.append(jnp.where(slot < live, cells_v[source, pl.ds(owner, 1), :], -1))
-    listed = jnp.concatenate(listed, axis=1)
-    tile = (lax.broadcasted_iota(jnp.int32, listed.shape, 1) // slots) % 3
-    bits = across.bit_length() - 1
-    at = jnp.where(listed < 0, -1, (listed >> bits) + (rows * (tile - 1) + PAD))
-    places[...] = jnp.broadcast_to(at, places.shape)
-    columns = listed & (across - 1)
-    hot[...] = jnp.where(lax.broadcasted_iota(jnp.int32, hot.shape, 0) == columns, 1.0, 0.0).astype(jnp.bfloat16)
-
-    for q in range(tiles // 2):
-        row, lane_at = packed(q, across)
-        values = residual_rows(met(me ^ 1, q, tiles), own)
-        edges[row : row + STEPS, lane_at : lane_at + 128] = jnp.concatenate(
-            [values, jnp.zeros((STEPS, 128 - values.shape[1]), jnp.float32)], axis=1
-        )
-
     for h in range(halves):
         large[2 * h].wait()
         hi, lo = split(eta_v[h].reshape(wide, across))
@@ -153,14 +129,16 @@
         start = rows - CEL_HALO if last else 0
         out[CEL_AT : CEL_AT + CEL_HALO, :] = cel[start : start + CEL_HALO, :]
 
-    @pl.when(me % 2 == 0)
+    odd = lax.axis_index("trench") % 2
+
+    @pl.when(odd == 0)
     def _():
-        edge(edges, True)
+        edge(inner, True)
         edge(outer, False)
 
-    @pl.when(me % 2 == 1)
+    @pl.when(odd == 1)
     def _():
-        edge(edges, False)
+        edge(inner, False)
         edge(outer, True)
 
 
@@ -179,31 +157,44 @@
     return jnp.concatenate([own[jnp.clip(owner + d - 1, 0, tiles - 1)] for d in range(3)], axis=1)
 
 
-def packed(q, across):
-    per = across // 128
-    return ROWS + STEPS * (q // per), 128 * (q % per)
-
-
-def both_rows(owner, q, own, edges):
-    row, lane_at = packed(q, edges.shape[1])
-    slots = own.shape[2]
-    return jnp.concatenate(
-        [residual_rows(owner, own), edges[row : row + STEPS, lane_at : lane_at + 3 * slots]], axis=1
-    )
-
-
-def relay_kernel(own, edges, outer, *outs):
+def both_rows(owner, own, partner):
+    return jnp.concatenate([residual_rows(owner, own), residual_rows(owner, partner)], axis=1)
+
+
+def relay_kernel(own, partner, outer, *outs):
     me = lax.axis_index("trench")
     tiles = own.shape[0]
     for d, out in enumerate(outs, 1):
-        values = both_rows(met(me, d, tiles), d, own, edges)
+        values = both_rows(met(me, d, tiles), own, partner)
         fill = jnp.zeros((STEPS, out.shape[1] - values.shape[1]), jnp.float32)
         out[0:STEPS, :] = jnp.concatenate([values, fill], axis=1)
         if d == 1:
             out[STEPS : STEPS + ROWS, :] = outer[...]
 
 
-def advance_kernel(blocks, fields, cel, coef, hot, places, own, edges, *refs):
+def sensors_kernel(rows, cells, count, hot, places):
+    me = lax.axis_index("trench")
+    tiles, _, slots = cells.shape
+    across = hot.shape[0]
+    slot = lax.broadcasted_iota(jnp.int32, (1, slots), 1)
+    listed = []
+    for source in sources(me, tiles):
+        for d in range(3):
+            owner = me + d - 1
+            inside = (owner >= 0) & (owner < tiles)
+            owner = jnp.clip(owner, 0, tiles - 1)
+            live = jnp.where(inside, count[source, owner], 0)
+            listed.append(jnp.where(slot < live, cells[source, pl.ds(owner, 1), :], -1))
+    listed = jnp.concatenate(listed, axis=1)
+    tile = (lax.broadcasted_iota(jnp.int32, listed.shape, 1) // slots) % 3
+    bits = across.bit_length() - 1
+    at = jnp.where(listed < 0, -1, (listed >> bits) + (rows * (tile - 1) + PAD))
+    places[...] = jnp.broadcast_to(at, places.shape)
+    columns = listed & (across - 1)
+    hot[...] = jnp.where(lax.broadcasted_iota(jnp.int32, hot.shape, 0) == columns, 1.0, 0.0).astype(jnp.bfloat16)
+
+
+def advance_kernel(blocks, fields, cel, coef, hot, places, own, partner, facing_in, *refs):
     cross, outs, (stage, ext, cel_ext) = refs[: -3 - blocks], refs[-3 - blocks : -3], refs[-3:]
     me = lax.axis_index("trench")
     tiles = own.shape[0]
@@ -212,7 +203,7 @@
     part = rows // blocks
     odd = me % 2 == 1
     facing = me // 2 + jnp.where(odd, 1, -1)
-    inner = edges[0:ROWS, :]
+    inner = facing_in[...]
     outer = jnp.zeros(inner.shape, jnp.float32)
     if cross:
         outer = jnp.where((facing >= 0) & (facing < tiles // 2), cross[0][STEPS : STEPS + ROWS, :], outer)
@@ -220,12 +211,12 @@
     after = jnp.where(odd, outer, inner)
 
     per = 6 * own.shape[2]
-    values = [both_rows(me, 0, own, edges)] + [got[0:STEPS, 0:per] for got in cross]
+    values = [both_rows(me, own, partner)] + [got[0:STEPS, 0:per] for got in cross]
     values = jnp.concatenate(values, axis=1)
     here = lax.broadcasted_iota(jnp.int32, (tall, values.shape[1]), 0) == places[0:1, :]
     left = jnp.concatenate([jnp.where(here, values[t : t + 1, :], 0.0) for t in range(STEPS)], axis=0)
-    hi, lo = split(left)
-    planes = dot(hi, hot[...], ((1,), (1,))) + dot(lo, hot[...], ((1,), (1,)))
+    planes = dot(jnp.concatenate(split(left), axis=0), hot[...], ((1,), (1,)))
+    planes = planes[: STEPS * tall] + planes[STEPS * tall :]
     inject = [planes[tall * t : tall * t + tall] for t in range(STEPS)]
 
     def extend(store, own, at, width):
@@ -278,17 +269,29 @@
 
 
 def prior_kernel(*refs):
-    gots, weight, out, whole = refs[:-3], refs[-3], refs[-2], refs[-1]
+    gots, (weight, out, whole, done, sems) = refs[:-5], refs[-5:]
     block = lax.axis_index("tblock")
     for r, got in enumerate(reversed(gots)):
         whole[block ^ r] = got[...]
     part = out.shape[1]
     length = out.shape[0]
     width = weight.shape[0]
+    factor = [weight[j : j + 1, :] for j in range(width)]
+    copies = []
+
+    def finish(p):
+        if (p + 1) % (length // 4) == 0:
+            cut = pl.ds(p + 1 - length // 4, length // 4)
+            copies.append(pltpu.make_async_copy(done.at[cut], out.at[cut], sems.at[len(copies)]))
+            copies[-1].start()
+
     if 2 * part != 8:
         series = [whole[i // STEPS, part * (i % STEPS) : part * (i % STEPS) + part, :] for i in range(length)]
         for k in range(length):
-            out[k] = sum(weight[j] * series[k + j] for j in range(min(width, length - k)))
+            done[k] = sum(factor[j] * series[k + j] for j in range(min(width, length - k)))
+            finish(k)
+        for copy in copies:
+            copy.wait()
         return
     pairs = length // 2
     even = [whole[p // 2, 8 * (p % 2) : 8 * (p % 2) + 8, :] for p in range(pairs)]
@@ -299,10 +302,13 @@
         total = None
         for j in range(width):
             if p + j // 2 < pairs:
-                term = weight[j] * (odd if j % 2 else even)[p + j // 2]
+                term = factor[j] * (odd if j % 2 else even)[p + j // 2]
                 total = term if total is None else total + term
-        out[2 * p] = total[:part]
-        out[2 * p + 1] = total[part:]
+        done[2 * p] = total[:part]
+        done[2 * p + 1] = total[part:]
+        finish(2 * p + 1)
+    for copy in copies:
+        copy.wait()
 
 
 def shape(*dims, dtype=jnp.float32):
@@ -346,18 +352,19 @@
         pairs = [(2 * c + 1, 2 * ((c + d) % chips)) for c in range(chips)]
         return lax.ppermute(x, "trench", pairs + [(j, i) for i, j in pairs])
 
-    fields, edges, outer, cel, coef, hot, places = pl.pallas_call(
+    partner = meet(own, 0)
+    fields, inner, outer, cel, coef, factor, own = pl.pallas_call(
         contract_kernel,
         out_shape=(
             shape(len(FIELDS), rows, across),
-            shape(ROWS + STEPS * -(-64 * tiles // across), across),
+            shape(ROWS, across),
             shape(ROWS, across),
             shape(rows, across),
             shape(8 * STEPS, across),
-            shape(across, lanes, dtype=jnp.bfloat16),
-            shape(8, lanes, dtype=jnp.int32),
+            shape(band_weight.shape[0], across),
+            shape(*own.shape),
         ),
-        in_specs=[spec(pltpu.HBM)] * 9,
+        in_specs=[spec(pltpu.HBM)] * 8,
         out_specs=(spec(VMEM),) * 7,
         scratch_shapes=[
             VMEM((rows // 8, levels, 8, across), jnp.float32),
@@ -366,10 +373,8 @@
             SMEM(speed_table.shape, jnp.float32),
             VMEM((1, levels), jnp.float32),
             VMEM((1, levels), jnp.float32),
-            VMEM(sensor_cell.shape, jnp.int32),
-            SMEM(sensor_count.shape, jnp.int32),
-            VMEM(own.shape, jnp.float32),
-            pltpu.SemaphoreType.DMA((7 + 2 * (rows // 8),)),
+            VMEM((1, band_weight.shape[0]), jnp.float32),
+            pltpu.SemaphoreType.DMA((6 + 2 * (rows // 8),)),
         ],
         compiler_params=params,
         cost_estimate=pl.CostEstimate(flops=10**9, bytes_accessed=10**7, transcendentals=0),
@@ -379,12 +384,11 @@
             pltpu.with_memory_space_constraint(x, pltpu.HBM)
             for x in (
                 adjoint_eta, adjoint_flow, depth_class, speed_table, damping[None], profile[None],
-                sensor_cell, sensor_count, own,
+                band_weight[None], own,
             )
         ]
     )
-
-    edges = meet(edges, 0)
+    facing_in = meet(inner, 0)
     relays = pl.pallas_call(
         relay_kernel,
         out_shape=[
@@ -395,12 +399,21 @@
         out_specs=[spec(VMEM)] * (chips - 1),
         compiler_params=params,
         name="relay",
-    )(own, edges, outer)
+    )(own, partner, outer)
     cross = [meet(relay, d) for d, relay in enumerate(relays, 1)]
+    hot, places = pl.pallas_call(
+        functools.partial(sensors_kernel, rows),
+        out_shape=(shape(across, lanes, dtype=jnp.bfloat16), shape(8, lanes, dtype=jnp.int32)),
+        in_specs=[spec(VMEM), spec(SMEM)],
+        out_specs=(spec(VMEM),) * 2,
+        compiler_params=params,
+        cost_estimate=pl.CostEstimate(flops=10**6, bytes_accessed=2 * 10**6, transcendentals=0),
+        name="sensors",
+    )(sensor_cell, sensor_count)
     series = pl.pallas_call(
         functools.partial(advance_kernel, blocks),
         out_shape=(shape(STEPS * rows // blocks, across),) * blocks,
-        in_specs=[spec(VMEM)] * (7 + len(cross)),
+        in_specs=[spec(VMEM)] * (8 + len(cross)),
         out_specs=(spec(VMEM),) * blocks,
         scratch_shapes=[
             VMEM((blocks, STEPS * rows // blocks, across), jnp.float32),
@@ -409,17 +422,21 @@
         ],
         compiler_params=params,
         name="advance",
-    )(fields, cel, coef, hot, places, own, edges, *cross)
+    )(fields, cel, coef, hot, places, own, partner, facing_in, *cross)
     gots = swaps(series, "tblock")
     return pl.pallas_call(
         prior_kernel,
         out_shape=shape(STEPS * blocks, rows // blocks, across),
-        in_specs=[spec(VMEM)] * blocks + [spec(SMEM)],
-        out_specs=spec(VMEM),
-        scratch_shapes=[VMEM((blocks, STEPS * rows // blocks, across), jnp.float32)],
+        in_specs=[spec(VMEM)] * (blocks + 1),
+        out_specs=spec(pl.ANY),
+        scratch_shapes=[
+            VMEM((blocks, STEPS * rows // blocks, across), jnp.float32),
+            VMEM((STEPS * blocks, rows // blocks, across), jnp.float32),
+            pltpu.SemaphoreType.DMA((4,)),
+        ],
         compiler_params=params,
         name="prior",
-    )(*reversed(gots), band_weight)
+    )(*reversed(gots), factor)
 
 
 def solution(mesh):

time: 22.3 us -> 20.5 us (0.919)
  waiting for transfers between devices: 7.75 us -> 5.9 us
    ppermute x4 -> x5, waiting for transfers between devices: 3.64 us -> 1.81 us  [meet(): return lax.ppermute(x, 'trench', pairs + [(j, i) for i, j in pairs])]
    pallas_call x0 -> x1, Pallas kernels: none -> 1.02 us  [body(): pl.pallas_call(functools.partial(sensors_kernel, rows), out_shape=(shape(...]
    pallas_call x1, Pallas kernels: 1.28 us -> 0.74 us  [body(): pl.pallas_call(prior_kernel, out_shape=shape(STEPS * blocks, rows // bloc...]
    pallas_call x1, Pallas kernels: 2.52 us -> 2.22 us  [body(): pl.pallas_call(contract_kernel, out_shape=(shape(len(FIELDS), rows, acros...]
    ppermute x4 -> x5, starting transfers between devices: 4.95 us -> 4.88 us  [meet(): return lax.ppermute(x, 'trench', pairs + [(j, i) for i, j in pairs])]
  transfers between devices with their start and end apart: 7 -> 8, of which waited for: 5 -> 4; matrix products, arithmetic and copies ran while one was open for 0% -> 0% of each run, Pallas kernels for 0% -> 16%
where the time goes in v1:
time: 20.5 us; the launch traced here: 20.3 us
  starting transfers between devices  9.34 us (46%)
  waiting for transfers between devices  5.9 us (29%)
  Pallas kernels  5.03 us (25%)
    ppermute x5, starting transfers between devices, meet(): return lax.ppermute(x, 'trench', pairs + [(j, i) for i, j in pairs])  4.88 us
    ppermute x3, starting transfers between devices, swaps(): lax.ppermute(parts[r], axis, [(i, i ^ r) for i in range(devices)])  4.45 us
    ppermute x3, waiting for transfers between devices, swaps(): lax.ppermute(parts[r], axis, [(i, i ^ r) for i in range(devices)])  4.08 us
    pallas_call x1, Pallas kernels, body(): pl.pallas_call(contract_kernel, out_shape=(shape(len(FIELDS), rows, acros...  2.22 us
    ppermute x5, waiting for transfers between devices, meet(): return lax.ppermute(x, 'trench', pairs + [(j, i) for i, j in pairs])  1.81 us
    pallas_call x1, Pallas kernels, body(): pl.pallas_call(functools.partial(sensors_kernel, rows), out_shape=(shape(...  1.02 us
    pallas_call x1, Pallas kernels, body(): pl.pallas_call(functools.partial(advance_kernel, blocks), out_shape=(shap...  0.87 us
    pallas_call x1, Pallas kernels, body(): pl.pallas_call(prior_kernel, out_shape=shape(STEPS * blocks, rows // bloc...  0.74 us
  transfers between devices with their start and end apart: 8, of which 4 were waited for; matrix products, arithmetic and copies ran while one was open for 0% of the time, Pallas kernels for 16%

profile of v1, /device:TPU:0, one launch (start us, length us, event | category | flops | bytes accessed | tf_op | source)
XLA Modules:
  0.0 20.3 jit_solution(11327694661439530580)
XLA Ops:
  0.0 0.5 %collective-permute-start = (f32[8,4,32]{2,1,0:T(4,128)}, f32[8,4,32]{2,1,0:T(4,128)S(1)}, u32[]{:S(2)}, u32[]{:S(2)}) collective-permute-start(f32[8,4,32]{2,1,0:T(4,128)} %bitcast.4), channel_id=1, source_target_pairs={{4,0},{12,8},{20,16},{28,24},{0,4},{8,12},{16,20},{24,28},{5,1},{1... | collective-permute-start | bytes 12296 | tf_op jit(solution)/shard_map/ppermute | solution.py:353
  0.5 2.2 %contract.1 = (f32[11,16,512]{2,1,0:T(8,128)S(1)}, f32[17,512]{1,0:T(8,128)S(1)}, f32[17,512]{1,0:T(8,128)S(1)}, f32[16,512]{1,0:T(8,128)S(1)}, f32[32,512]{1,0:...) custom-call(f32[1,30,16,512]{3,2,1,0:T(8,128)} %eta.1, f32[1,30,16,512]{3,2,1,0:T(8,128)} %flow.1, ...), custom_call_target="tpu_custom_call" | custom-call | flops 1000000000 | bytes 10000000 | tf_op jit(solution)/shard_map/contract/pallas_call | solution.py:356
  2.7 0.0 collective-permute-done.partner
  2.7 0.0 copy-start
  2.7 0.2 relay.1
  2.9 3.6 %collective-permute-start.2 = (f32[21,512]{1,0:T(8,128)S(1)}, f32[21,512]{1,0:T(8,128)S(1)}, u32[]{:S(2)}, u32[]{:S(2)}) collective-permute-start(f32[21,512]{1,0:T(8,128)S(1)} %get-tuple-element.29), channel_id=1, source_target_pairs={{4,8},{12,16},{20,24},{28,0},{8,4},{16,12},{24,20},{0,28},{5,9},{1... | collective-permute-start | bytes 129032 | tf_op jit(solution)/shard_map/ppermute | solution.py:353
  6.5 0.0 collective-permute-start.1
  6.5 0.6 %collective-permute-start.3 = (f32[4,256]{1,0:T(4,128)S(1)}, f32[4,256]{1,0:T(4,128)S(1)}, u32[]{:S(2)}, u32[]{:S(2)}) collective-permute-start(f32[4,256]{1,0:T(4,128)S(1)} %get-tuple-element.30), channel_id=1, source_target_pairs={{4,16},{12,24},{20,0},{28,8},{16,4},{24,12},{0,20},{8,28},{5,17},{... | collective-permute-start | bytes 12296 | tf_op jit(solution)/shard_map/ppermute | solution.py:353
  7.1 0.2 collective-permute-start.4
  7.3 0.0 copy-done
  7.3 0.0 copy-done.1
  7.3 1.0 %sensors.1 = (bf16[512,768]{1,0:T(8,128)(2,1)S(1)}, s32[8,768]{1,0:T(8,128)S(1)}) custom-call(s32[8,8,32]{2,1,0:T(8,128)S(1)} %copy-done, s32[8,8]{1,0:T(8,128)S(1)} %copy-done.1), custom_call_target="tpu_custom_call" | custom-call | flops 1000000 | bytes 2000000 | tf_op jit(solution)/shard_map/sensors/pallas_call | solution.py:404
  8.3 1.2 %collective-permute-done.3.refs_1_ = f32[4,256]{1,0:T(4,128)S(1)} collective-permute-done((f32[4,256]{1,0:T(4,128)S(1)}, f32[4,256]{1,0:T(4,128)S(1)}, u32[]{:S(2)}, u32[]{:S(2)}) %collective-permute-start.3) | collective-permute-done | bytes 4128 | tf_op jit(solution)/shard_map/ppermute | solution.py:353
  9.5 0.6 %collective-permute-done.4.refs_2_ = f32[4,256]{1,0:T(4,128)S(1)} collective-permute-done((f32[4,256]{1,0:T(4,128)S(1)}, f32[4,256]{1,0:T(4,128)S(1)}, u32[]{:S(2)}, u32[]{:S(2)}) %collective-permute-start.4) | collective-permute-done | bytes 4128 | tf_op jit(solution)/shard_map/ppermute | solution.py:353
  10.2 0.0 collective-permute-done.1.facing_in
  10.2 0.0 collective-permute-done.2.refs_0_
  10.2 0.9 %advance.1 = (f32[16,512]{1,0:T(8,128)S(1)}, f32[16,512]{1,0:T(8,128)S(1)}, f32[16,512]{1,0:T(8,128)S(1)}, f32[16,512]{1,0:T(8,128)S(1)}) custom-call(f32[11,16,512]{2,1,0:T(8,128)S(1)} %get-tuple-element.21.fields, f32[16,512]{1,0:T(8,128)S(1)} %get-tuple-element.22.cel, f32[32,512]{1,0:T(8,128)S(1)} %get-tuple-element.23.coef, ...), custom_call_target="tpu_custom_call" | custom-call | tf_op jit(solution)/shard_map/advance/pallas_call | solution.py:413
  11.0 3.7 %collective-permute-start.5 = (f32[16,512]{1,0:T(8,128)S(1)}, f32[16,512]{1,0:T(8,128)S(1)}, u32[]{:S(2)}, u32[]{:S(2)}) collective-permute-start(f32[16,512]{1,0:T(8,128)S(1)} %get-tuple-element.32), channel_id=1, source_target_pairs={{0,3},{1,2},{2,1},{3,0},{4,7},{5,6},{6,5},{7,4},{8,11},{9,10},{10,... | collective-permute-start | bytes 98312 | tf_op jit(solution)/shard_map/ppermute | solution.py:342
  14.7 0.0 collective-permute-start.6
  14.7 0.8 %collective-permute-start.7 = (f32[16,512]{1,0:T(8,128)S(1)}, f32[16,512]{1,0:T(8,128)S(1)}, u32[]{:S(2)}, u32[]{:S(2)}) collective-permute-start(f32[16,512]{1,0:T(8,128)S(1)} %get-tuple-element.34), channel_id=1, source_target_pairs={{0,1},{1,0},{2,3},{3,2},{4,5},{5,4},{6,7},{7,6},{8,9},{9,8},{10,11... | collective-permute-start | bytes 98312 | tf_op jit(solution)/shard_map/ppermute | solution.py:342
  15.5 1.6 %collective-permute-done.5.refs_0_ = f32[16,512]{1,0:T(8,128)S(1)} collective-permute-done((f32[16,512]{1,0:T(8,128)S(1)}, f32[16,512]{1,0:T(8,128)S(1)}, u32[]{:S(2)}, u32[]{:S(2)}) %collective-permute-start.5) | collective-permute-done | bytes 32800 | tf_op jit(solution)/shard_map/ppermute | solution.py:342
  17.1 2.5 %collective-permute-done.6.refs_1_ = f32[16,512]{1,0:T(8,128)S(1)} collective-permute-done((f32[16,512]{1,0:T(8,128)S(1)}, f32[16,512]{1,0:T(8,128)S(1)}, u32[]{:S(2)}, u32[]{:S(2)}) %collective-permute-start.6) | collective-permute-done | bytes 32800 | tf_op jit(solution)/shard_map/ppermute | solution.py:342
  19.6 0.0 collective-permute-done.7.refs_2_
  19.6 0.7 %prior.1 = f32[16,4,512]{2,1,0:T(4,128)} custom-call(f32[16,512]{1,0:T(8,128)S(1)} %collective-permute-done.5.refs_0_, f32[16,512]{1,0:T(8,128)S(1)} %collective-permute-done.6.refs_1_, f32[16,512]{1,0:T(8,128)S(1)} %collective-permute-done.7.refs_2_, f32[16,512]{1,0:T(8,128)S(1)} %get-tuple-element.35.refs_3_, f32[8,512]{1,0:T(8,128)S(1)} %get-tuple-element.36.refs_4_), custom_call_target="tpu_custom_call" | custom-call | tf_op jit(solution)/shard_map/prior/pallas_call | solution.py:427
  (1 shorter events, 0.0 us)
Async XLA Ops:
  0.0 2.7 %collective-permute-start = (f32[8,4,32]{2,1,0:T(4,128)}, f32[8,4,32]{2,1,0:T(4,128)S(1)}, u32[]{:S(2)}, u32[]{:S(2)}) collective-permute-start(f32[8,4,32]{2,1,0:T(4,128)} %bitcast.4), channel_id=1, source_target_pairs={{4,0},{12,8},{20,16},{28,24},{0,4},{8,12},{16,20},{24,28},{5,1},{1... | collective-permute-start | bytes 12296 | tf_op jit(solution)/shard_map/ppermute | solution.py:353
  2.7 4.6 %copy-start = (s32[8,8,32]{2,1,0:T(8,128)S(1)}, s32[8,8,32]{2,1,0:T(8,128)}, u32[]{:S(2)}) copy-start(s32[8,8,32]{2,1,0:T(8,128)} %cells.1) | copy-start | bytes 24580
  2.9 4.4 %copy-start.1 = (s32[8,8]{1,0:T(8,128)S(1)}, s32[8,8]{1,0:T(8,128)}, u32[]{:S(2)}) copy-start(s32[8,8]{1,0:T(8,128)} %count.1) | copy-start | bytes 772
  2.9 7.3 %collective-permute-start.2 = (f32[21,512]{1,0:T(8,128)S(1)}, f32[21,512]{1,0:T(8,128)S(1)}, u32[]{:S(2)}, u32[]{:S(2)}) collective-permute-start(f32[21,512]{1,0:T(8,128)S(1)} %get-tuple-element.29), channel_id=1, source_target_pairs={{4,8},{12,16},{20,24},{28,0},{8,4},{16,12},{24,20},{0,28},{5,9},{1... | collective-permute-start | bytes 129032 | tf_op jit(solution)/shard_map/ppermute | solution.py:353
  6.5 3.7 %collective-permute-start.1 = (f32[17,512]{1,0:T(8,128)S(1)}, f32[17,512]{1,0:T(8,128)S(1)}, u32[]{:S(2)}, u32[]{:S(2)}) collective-permute-start(f32[17,512]{1,0:T(8,128)S(1)} %get-tuple-element.27), channel_id=1, source_target_pairs={{4,0},{12,8},{20,16},{28,24},{0,4},{8,12},{16,20},{24,28},{5,1},{1... | collective-permute-start | bytes 104456 | tf_op jit(solution)/shard_map/ppermute | solution.py:353
  6.5 3.0 %collective-permute-start.3 = (f32[4,256]{1,0:T(4,128)S(1)}, f32[4,256]{1,0:T(4,128)S(1)}, u32[]{:S(2)}, u32[]{:S(2)}) collective-permute-start(f32[4,256]{1,0:T(4,128)S(1)} %get-tuple-element.30), channel_id=1, source_target_pairs={{4,16},{12,24},{20,0},{28,8},{16,4},{24,12},{0,20},{8,28},{5,17},{... | collective-permute-start | bytes 12296 | tf_op jit(solution)/shard_map/ppermute | solution.py:353
  7.1 3.0 %collective-permute-start.4 = (f32[4,256]{1,0:T(4,128)S(1)}, f32[4,256]{1,0:T(4,128)S(1)}, u32[]{:S(2)}, u32[]{:S(2)}) collective-permute-start(f32[4,256]{1,0:T(4,128)S(1)} %get-tuple-element.31), channel_id=1, source_target_pairs={{4,24},{12,0},{20,8},{28,16},{24,4},{0,12},{8,20},{16,28},{5,25},{... | collective-permute-start | bytes 12296 | tf_op jit(solution)/shard_map/ppermute | solution.py:353
  11.0 6.1 %collective-permute-start.5 = (f32[16,512]{1,0:T(8,128)S(1)}, f32[16,512]{1,0:T(8,128)S(1)}, u32[]{:S(2)}, u32[]{:S(2)}) collective-permute-start(f32[16,512]{1,0:T(8,128)S(1)} %get-tuple-element.32), channel_id=1, source_target_pairs={{0,3},{1,2},{2,1},{3,0},{4,7},{5,6},{6,5},{7,4},{8,11},{9,10},{10,... | collective-permute-start | bytes 98312 | tf_op jit(solution)/shard_map/ppermute | solution.py:342
  14.7 4.9 %collective-permute-start.6 = (f32[16,512]{1,0:T(8,128)S(1)}, f32[16,512]{1,0:T(8,128)S(1)}, u32[]{:S(2)}, u32[]{:S(2)}) collective-permute-start(f32[16,512]{1,0:T(8,128)S(1)} %get-tuple-element.33), channel_id=1, source_target_pairs={{0,2},{1,3},{2,0},{3,1},{4,6},{5,7},{6,4},{7,5},{8,10},{9,11},{10,... | collective-permute-start | bytes 98312 | tf_op jit(solution)/shard_map/ppermute | solution.py:342
  14.7 4.9 %collective-permute-start.7 = (f32[16,512]{1,0:T(8,128)S(1)}, f32[16,512]{1,0:T(8,128)S(1)}, u32[]{:S(2)}, u32[]{:S(2)}) collective-permute-start(f32[16,512]{1,0:T(8,128)S(1)} %get-tuple-element.34), channel_id=1, source_target_pairs={{0,1},{1,0},{2,3},{3,2},{4,5},{5,4},{6,7},{7,6},{8,9},{9,8},{10,11... | collective-permute-start | bytes 98312 | tf_op jit(solution)/shard_map/ppermute | solution.py:342
